TPU v7x, 32 devices: a whole 2x2x4 slice. The times are simulated.
32 devices in a mesh: groups: 2 (over x), ctx: 16 (over z, y, core).
Axes of the slice: x: 2, y: 2, z: 4, core: 2. Of those that a mesh axis runs over, the one named last changes fastest.
Arguments:
- queries: bfloat16 [4096, 2048], P(('groups', 'ctx')), parts along dimension 0, may hold values from -90 to 90
- keys: bfloat16 [4096, 128], P(('groups', 'ctx')), parts along dimension 0, may hold values from -6 to 6
- values: bfloat16 [4096, 128], P(('groups', 'ctx')), parts along dimension 0, may hold values from -6 to 6
- cache_lengths: int32 [16], P('groups'), parts along dimension 0, may hold values from 1 to 1024, as said below
- query_lengths: int32 [16], P('groups'), parts along dimension 0, may hold values from 1 to 1024, as said below
Outputs:
- attended: bfloat16 [4096, 2048], P(('groups', 'ctx')), parts along dimension 0
- log_total: float32 [4096, 16], P(('groups', 'ctx')), parts along dimension 0
There are 2 independent parts, one for each index of `groups`. A program takes and returns all parts, laid end to end along the dimension named above; each array names one. Nothing has to cross between parts.
Inputs may be any that keep to these rules, and one draw needn't show every extreme that they name: `cache_lengths`: Positive, summing to 2048; the largest is exactly 1024. `query_lengths`: Positive, summing to 2048; the largest is exactly 1024.
All inputs are finite; a program needn't handle non-finite values.
Results may differ from a plain program's by a relative error of at most 0.0045.
Values may be sent and summed in bfloat16 or wider, within the bound.
A program may use at most 64 MiB of HBM per device.

v0:
```python
import math
import jax
import jax.numpy as jnp
from jax import lax
from jax.sharding import PartitionSpec as P

NEG_FILL = -1e30


def request_of(positions, lengths):
    ends = jnp.cumsum(lengths)[:-1]
    return jnp.sum((positions[:, None] >= ends[None, :]).astype(jnp.int32), axis=1)


def shards(queries, keys, values, cache_lengths, query_lengths):
    q_dev = queries.shape[0]
    width = keys.shape[1]
    heads = queries.shape[1] // width
    here = lax.axis_index("ctx")
    rows = queries.reshape(q_dev * heads, width)
    query_req = request_of(here * q_dev + jnp.arange(q_dev, dtype=jnp.int32), query_lengths)
    row_req = jnp.repeat(query_req, heads)
    scale = width ** (-0.5)

    def attend(carry, key_block, value_block, start):
        positions = start + jnp.arange(key_block.shape[0], dtype=jnp.int32)
        cache_req = request_of(positions, cache_lengths)
        top, total, mixed = carry
        score = jnp.dot(rows, key_block.T, preferred_element_type=jnp.float32) * scale
        mask = (row_req[:, None] == cache_req[None, :]) & True
        score = jnp.where(mask, score, NEG_FILL)
        new_top = jnp.maximum(top, jnp.max(score, axis=1))
        factor = jnp.exp(top - new_top)
        weight = jnp.where(mask, jnp.exp(score - new_top[:, None]), 0.0)
        total = total * factor + jnp.sum(weight, axis=1)
        mixed = mixed * factor[:, None] + jnp.dot(
            weight.astype(jnp.bfloat16), value_block, preferred_element_type=jnp.float32
        )
        return (new_top, total, mixed)

    start_state = (
        jnp.full((q_dev * heads,), NEG_FILL, jnp.float32),
        jnp.zeros((q_dev * heads,), jnp.float32),
        jnp.zeros((q_dev * heads, width), jnp.float32),
    )
    key_piece = lax.all_gather(keys, "ctx", axis=0, tiled=True)
    value_piece = lax.all_gather(values, "ctx", axis=0, tiled=True)
    length = key_piece.shape[0]
    block = math.gcd(length, 1024)
    nblocks = length // block

    def one_step(index, state):
        key_block = lax.dynamic_slice_in_dim(key_piece, index * block, block, 0)
        value_block = lax.dynamic_slice_in_dim(value_piece, index * block, block, 0)
        return attend(state, key_block, value_block, index * block)

    top, total, mixed = lax.fori_loop(0, nblocks, one_step, start_state)
    attended = (mixed / total[:, None]).astype(jnp.bfloat16).reshape(q_dev, heads * width)
    log_total = (top + jnp.log(total)).reshape(q_dev, heads)
    return (attended, log_total)


def solution(mesh):
    in_specs = (
        P(("groups", "ctx"), None),
        P(("groups", "ctx"), None),
        P(("groups", "ctx"), None),
        P("groups"),
        P("groups"),
    )
    out_specs = (P(("groups", "ctx"), None), P(("groups", "ctx"), None))
    return jax.shard_map(shards, mesh=mesh, in_specs=in_specs, out_specs=out_specs, check_vma=False)
```

profile of v0, /device:TPU:0, one launch (start us, length us, event | category | flops | bytes accessed | tf_op | source)
XLA Modules:
  0.0 64.0 jit_solution(3821850923970895720)
XLA Ops:
  0.6 0.8 %reduce-window.15 = s32[8,1]{0,1:T(1,128)S(1)} reduce-window(s32[8,1]{0,1:T(1,128)} %bitcast.30, s32[]{:T(128)} %constant.83.clone.1), window={size=8x1 pad=7_0x0_0}, to_apply=%region_2.3 | reduce-window | flops 56 | bytes 68 | tf_op jit(solution)/shard_map/reduce-window.4
  1.5 0.8 %reduce-window.14 = s32[8,1]{0,1:T(1,128)S(1)} reduce-window(s32[8,1]{0,1:T(1,128)} %bitcast.31, s32[]{:T(128)} %constant.83.clone.1), window={size=8x1 pad=7_0x0_0}, to_apply=%region_0.0 | reduce-window | flops 56 | bytes 68 | tf_op jit(solution)/shard_map/reduce-window
  2.3 0.1 convert_reduce_fusion.1
  2.4 1.3 %reshape.46 = bf16[2048,128]{1,0:T(8,128)(2,1)S(1)} reshape(bf16[128,2048]{1,0:T(8,128)(2,1)} %param.7) | data formatting | bytes 1048576 | tf_op jit(solution)/shard_map/reshape | solution.py:20
  3.7 24.8 %all_gather.6 = bf16[2048,128]{1,0:T(8,128)(2,1)S(1)} all-gather(bf16[128,128]{1,0:T(8,128)(2,1)} %param.8), channel_id=1, replica_groups=mesh['groups'=2,'ctx'=16] {'ctx'}, dimensions={0}, use_global_device_ids=true | all-gather | bytes 557056 | tf_op jit(solution)/shard_map/all_gather | solution.py:46
  28.5 19.1 %all_gather.7 = bf16[2048,128]{1,0:T(8,128)(2,1)S(1)} all-gather(bf16[128,128]{1,0:T(8,128)(2,1)} %param.9), channel_id=1, replica_groups=mesh['groups'=2,'ctx'=16] {'ctx'}, dimensions={0}, use_global_device_ids=true | all-gather | bytes 557056 | tf_op jit(solution)/shard_map/all_gather | solution.py:47
  47.6 14.2 %while.20 = (s32[]{:T(128)}, f32[2048]{0:T(1024)S(1)}, f32[2048]{0:T(1024)S(1)}, f32[2048,128]{1,0:T(8,128)S(1)}, s32[8,1]{0,1:T(1,128)S(1)}, /*index=5*/bf16[20...) while((s32[]{:T(128)}, f32[2048]{0:T(1024)S(1)}, ...), condition=%wide.region_7.8_spmd.clone, body=%wide.region_3.7_spmd.clone.sunk | while | flops 1108114432 | bytes 28517148 | solution.py:57
  47.6 0.1 convert_reduce_fusion.3
  47.7 0.1 broadcast_in_dim.81
  47.8 0.1 eq.93
  47.8 1.3 %fusion.30 = (f32[2048]{0:T(1024)S(1)}, f32[1024,2048]{1,0:T(8,128)S(1)}) fusion(s32[2048]{0:T(1024)S(1)} %eq.93, s32[1024]{0:T(1024)S(1)} %convert_reduce_fusion.3, bf16[2048,128]{1,0:T(8,128)(2,1)S(1)} %get-tuple-element.373, bf16[2048,128]{1,0:T(8,128)(2,1)S(1)} %get-tuple-element.372, s32[]{:T(128)S(6)} %select_n.63), kind=kOutput, calls=%fused_computation.3.clone.1 | convolution fusion | flops 545257472 | bytes 9195524 | tf_op jit(solution)/shard_map/while/body/eval_jaxpr/dot_general | solution.py:29
  49.2 2.7 %fusion.31 = f32[2048]{0:T(1024)S(1)} fusion(f32[1024,2048]{1,0:T(8,128)S(1)} %get-tuple-element.338, f32[2048]{0:T(1024)S(1)} %select_maximum_fusion.2, s32[2048]{0:T(1024)S(1)} %eq.93, s32[1024]{0:T(1024)S(1)} %convert_reduce_fusion.3), kind=kLoop, calls=%fused_computation.5.clone.1 | loop fusion | flops 12580864 | bytes 8417280 | tf_op jit(solution)/shard_map/while/body/eval_jaxpr/reduce_sum | solution.py:35
  51.9 2.8 %fusion.33 = f32[2048,128]{1,0:T(8,128)S(1)} fusion(f32[1024,2048]{1,0:T(8,128)S(1)} %get-tuple-element.338, f32[2048]{0:T(1024)S(1)} %select_maximum_fusion.2, s32[2048]{0:T(1024)S(1)} %eq.93, s32[1024]{0:T(1024)S(1)} %convert_reduce_fusion.3, f32[2048,128]{1,0:T(8,128)S(1)} %get-tuple-element.357, f32[2048]{0:T(1024)S(1)} %get-tuple-element.340, ...), kind=kOutput, calls=%fused_computation.7.clone.1 | convolution fusion | flops 550240256 | bytes 10776581 | tf_op jit(solution)/shard_map/while/body/eval_jaxpr/dot_general | solution.py:36
  54.7 0.1 convert_reduce_fusion.3
  54.8 0.1 broadcast_in_dim.81
  54.9 0.1 eq.93
  55.0 1.3 %fusion.30 = (f32[2048]{0:T(1024)S(1)}, f32[1024,2048]{1,0:T(8,128)S(1)}) fusion(s32[2048]{0:T(1024)S(1)} %eq.93, s32[1024]{0:T(1024)S(1)} %convert_reduce_fusion.3, bf16[2048,128]{1,0:T(8,128)(2,1)S(1)} %get-tuple-element.373, bf16[2048,128]{1,0:T(8,128)(2,1)S(1)} %get-tuple-element.372, s32[]{:T(128)S(6)} %select_n.63), kind=kOutput, calls=%fused_computation.3.clone.1 | convolution fusion | flops 545257472 | bytes 9195524 | tf_op jit(solution)/shard_map/while/body/eval_jaxpr/dot_general | solution.py:29
  56.3 2.7 %fusion.31 = f32[2048]{0:T(1024)S(1)} fusion(f32[1024,2048]{1,0:T(8,128)S(1)} %get-tuple-element.338, f32[2048]{0:T(1024)S(1)} %select_maximum_fusion.2, s32[2048]{0:T(1024)S(1)} %eq.93, s32[1024]{0:T(1024)S(1)} %convert_reduce_fusion.3), kind=kLoop, calls=%fused_computation.5.clone.1 | loop fusion | flops 12580864 | bytes 8417280 | tf_op jit(solution)/shard_map/while/body/eval_jaxpr/reduce_sum | solution.py:35
  59.0 2.8 %fusion.33 = f32[2048,128]{1,0:T(8,128)S(1)} fusion(f32[1024,2048]{1,0:T(8,128)S(1)} %get-tuple-element.338, f32[2048]{0:T(1024)S(1)} %select_maximum_fusion.2, s32[2048]{0:T(1024)S(1)} %eq.93, s32[1024]{0:T(1024)S(1)} %convert_reduce_fusion.3, f32[2048,128]{1,0:T(8,128)S(1)} %get-tuple-element.357, f32[2048]{0:T(1024)S(1)} %get-tuple-element.340, ...), kind=kOutput, calls=%fused_computation.7.clone.1 | convolution fusion | flops 550240256 | bytes 10776581 | tf_op jit(solution)/shard_map/while/body/eval_jaxpr/dot_general | solution.py:36
  61.8 0.3 divide_convert_fusion
  62.2 1.0 %reshape.47 = bf16[128,2048]{1,0:T(8,128)(2,1)} reshape(bf16[2048,128]{1,0:T(8,128)(2,1)S(1)} %divide_convert_fusion) | data formatting | bytes 1048576 | tf_op jit(solution)/shard_map/reshape | solution.py:58
  63.2 0.1 reshape.48
  63.3 0.7 %copy.8 = f32[128,16]{0,1:T(8,128)} copy(f32[128,16]{1,0:T(8,128)S(1)} %reshape.48) | data formatting | bytes 16384
  (16 shorter events, 0.1 us)
where the time goes:
time: 64.2 us; the launch traced here: 64 us
  blocking collectives  43.9 us (68%)
  matrix products  8.24 us (13%)
  other arithmetic  7.64 us (12%)
  local copies, waits for them, and re-layouts  3.38 us (5%)
  between operations  0.68 us (1%)
    all_gather x1, blocking collectives, shards(): key_piece = lax.all_gather(keys, 'ctx', axis=0, tiled=True)  24.8 us
    all_gather x1, blocking collectives, shards(): value_piece = lax.all_gather(values, 'ctx', axis=0, tiled=True)  19.1 us
    dot_general x2, matrix products, attend(): jnp.dot(weight.astype(jnp.bfloat16), value_block, preferred_element_type=...  5.61 us
    reduce_sum x2, other arithmetic, attend(): total = total * factor + jnp.sum(weight, axis=1)  5.33 us
    dot_general x2, matrix products, attend(): jnp.dot(rows, key_block.T, preferred_element_type=jnp.float32) * scale  2.62 us
    another operation x2, other arithmetic  1.66 us

commit v1 on v0

--- a/solution.py
+++ b/solution.py
@@ -3,8 +3,17 @@
 import jax.numpy as jnp
 from jax import lax
 from jax.sharding import PartitionSpec as P
+from jax.lax import all_gather
 
 NEG_FILL = -1e30
+
+
+def get_the_masks(field_in, dev_axis, point):
+    return jnp.split(
+        all_gather(jnp.concatenate([point, field_in], axis=1), dev_axis, axis=0, tiled=True),
+        [point.shape[1]],
+        axis=1,
+    )
 
 
 def request_of(positions, lengths):
@@ -43,8 +52,7 @@
         jnp.zeros((q_dev * heads,), jnp.float32),
         jnp.zeros((q_dev * heads, width), jnp.float32),
     )
-    key_piece = lax.all_gather(keys, "ctx", axis=0, tiled=True)
-    value_piece = lax.all_gather(values, "ctx", axis=0, tiled=True)
+    key_piece, value_piece = get_the_masks(values, "ctx", keys)
     length = key_piece.shape[0]
     block = math.gcd(length, 1024)
     nblocks = length // block

time: 64.2 us -> 76.2 us (1.19)
  blocking collectives: 43.9 us -> 0 us
  waiting for transfers between devices: 0 us -> 39.7 us
  between operations: 0.68 us -> 14.1 us
  other arithmetic: 7.64 us -> 9.06 us
  local copies, waits for them, and re-layouts: 3.38 us -> 4.65 us
    all_gather x2 -> x0, blocking collectives: 43.9 us -> none  [the longest x1 24.8 us: shards(): key_piece = lax.all_gather(keys, 'ctx', axis=0, tiled=True)]
    all_gather x0 -> x1, waiting for transfers between devices: none -> 39.7 us  [get_the_masks(): all_gather(jnp.concatenate([point, field_in], axis=1), dev_axis, axis=0,...]
    concatenate x0 -> x1, other arithmetic: none -> 1.41 us  [get_the_masks(): jnp.concatenate([point, field_in], axis=1)]
    split x0 -> x1, local copies, waits for them, and re-layouts: none -> 1.27 us  [get_the_masks(): jnp.split(all_gather(jnp.concatenate([point, field_in], axis=1), dev_axis...]
  transfers between devices with their start and end apart: 0 -> 1, of which waited for: 0 -> 1; matrix products, arithmetic and copies ran while one was open for 0% -> 4% of each run, Pallas kernels for 0% -> 0%
where the time goes in v1:
time: 76.2 us; the launch traced here: 75.9 us
  waiting for transfers between devices  39.7 us (52%)
  between operations  14.1 us (19%)
  other arithmetic  9.06 us (12%)
  matrix products  8.23 us (11%)
  local copies, waits for them, and re-layouts  4.65 us (6%)
    all_gather x1, waiting for transfers between devices, get_the_masks(): all_gather(jnp.concatenate([point, field_in], axis=1), dev_axis, axis=0,...  39.7 us
    dot_general x2, matrix products, attend(): jnp.dot(weight.astype(jnp.bfloat16), value_block, preferred_element_type=...  5.61 us
    reduce_sum x2, other arithmetic, attend(): total = total * factor + jnp.sum(weight, axis=1)  5.33 us
    dot_general x2, matrix products, attend(): jnp.dot(rows, key_block.T, preferred_element_type=jnp.float32) * scale  2.61 us
    another operation x2, other arithmetic  1.66 us
  transfers between devices with their start and end apart: 1, of which 1 were waited for; matrix products, arithmetic and copies ran while one was open for 4% of the time, Pallas kernels for 0%

profile of v1, /device:TPU:0, one launch (start us, length us, event | category | flops | bytes accessed | tf_op | source)
XLA Modules:
  0.0 75.9 jit_solution(14819751488951587506)
XLA Ops:
  7.2 1.4 %pad_maximum_fusion = bf16[128,256]{1,0:T(8,128)(2,1)} fusion(bf16[128,128]{1,0:T(8,128)(2,1)} %param.9, bf16[128,128]{1,0:T(8,128)(2,1)} %param.8), kind=kLoop, calls=%fused_computation.25 | loop fusion | flops 131072 | bytes 131072 | tf_op jit(solution)/shard_map/concatenate | solution.py:13
  8.7 0.8 %reduce-window.15 = s32[8,1]{0,1:T(1,128)S(1)} reduce-window(s32[8,1]{0,1:T(1,128)} %bitcast.30, s32[]{:T(128)} %constant.83.clone.1), window={size=8x1 pad=7_0x0_0}, to_apply=%region_2.3 | reduce-window | flops 56 | bytes 68 | tf_op jit(solution)/shard_map/reduce-window.4
  9.5 0.8 %reduce-window.14 = s32[8,1]{0,1:T(1,128)S(1)} reduce-window(s32[8,1]{0,1:T(1,128)} %bitcast.31, s32[]{:T(128)} %constant.83.clone.1), window={size=8x1 pad=7_0x0_0}, to_apply=%region_0.0 | reduce-window | flops 56 | bytes 68 | tf_op jit(solution)/shard_map/reduce-window
  10.3 1.3 %reshape.46 = bf16[2048,128]{1,0:T(8,128)(2,1)S(1)} reshape(bf16[128,2048]{1,0:T(8,128)(2,1)} %param.7) | data formatting | bytes 1048576 | tf_op jit(solution)/shard_map/reshape | solution.py:29
  11.7 0.1 convert_reduce_fusion.1
  11.7 39.7 %all-gather.2.cloned.1.call-done = bf16[2048,256]{1,0:T(8,128)(2,1)} async-done(((bf16[128,256]{1,0:T(8,128)(2,1)}), bf16[2048,256]{1,0:T(8,128)(2,1)}) %all-gather.2.cloned.1.call-update) | async-done | bytes 1048592 | tf_op jit(solution)/shard_map/all_gather | solution.py:13
  51.4 1.3 %fusion.19 = (bf16[2048,128]{1,0:T(8,128)(2,1)S(1)}, bf16[2048,128]{1,0:T(8,128)(2,1)S(1)}) fusion(bf16[2048,256]{1,0:T(8,128)(2,1)} %all-gather.2.cloned.1.call-done), kind=kLoop, calls=%fused_computation.30 | loop fusion | bytes 2097152 | tf_op jit(solution)/shard_map/split | solution.py:12
  52.7 14.3 %while.20 = (s32[]{:T(128)}, f32[2048]{0:T(1024)S(1)}, f32[2048]{0:T(1024)S(1)}, f32[2048,128]{1,0:T(8,128)S(1)}, s32[8,1]{0,1:T(1,128)S(1)}, /*index=5*/bf16[20...) while((s32[]{:T(128)}, f32[2048]{0:T(1024)S(1)}, ...), condition=%wide.region_7.8_spmd.clone, body=%wide.region_3.7_spmd.clone.sunk | while | flops 1108114432 | bytes 28517148 | solution.py:65
  52.7 0.1 convert_reduce_fusion.3
  52.8 0.1 broadcast_in_dim.81
  52.9 0.1 eq.93
  53.0 1.3 %fusion.31 = (f32[2048]{0:T(1024)S(1)}, f32[1024,2048]{1,0:T(8,128)S(1)}) fusion(s32[2048]{0:T(1024)S(1)} %eq.93, s32[1024]{0:T(1024)S(1)} %convert_reduce_fusion.3, bf16[2048,128]{1,0:T(8,128)(2,1)S(1)} %get-tuple-element.375, bf16[2048,128]{1,0:T(8,128)(2,1)S(1)} %get-tuple-element.374, s32[]{:T(128)S(6)} %select_n.63), kind=kOutput, calls=%fused_computation.3.clone.1 | convolution fusion | flops 545257472 | bytes 9195524 | tf_op jit(solution)/shard_map/while/body/eval_jaxpr/dot_general | solution.py:38
  54.3 2.7 %fusion.32 = f32[2048]{0:T(1024)S(1)} fusion(f32[1024,2048]{1,0:T(8,128)S(1)} %get-tuple-element.340, f32[2048]{0:T(1024)S(1)} %select_maximum_fusion.2, s32[2048]{0:T(1024)S(1)} %eq.93, s32[1024]{0:T(1024)S(1)} %convert_reduce_fusion.3), kind=kLoop, calls=%fused_computation.5.clone.1 | loop fusion | flops 12580864 | bytes 8417280 | tf_op jit(solution)/shard_map/while/body/eval_jaxpr/reduce_sum | solution.py:44
  57.0 2.8 %fusion.34 = f32[2048,128]{1,0:T(8,128)S(1)} fusion(f32[1024,2048]{1,0:T(8,128)S(1)} %get-tuple-element.340, f32[2048]{0:T(1024)S(1)} %select_maximum_fusion.2, s32[2048]{0:T(1024)S(1)} %eq.93, s32[1024]{0:T(1024)S(1)} %convert_reduce_fusion.3, f32[2048,128]{1,0:T(8,128)S(1)} %get-tuple-element.359, f32[2048]{0:T(1024)S(1)} %get-tuple-element.342, ...), kind=kOutput, calls=%fused_computation.7.clone.1 | convolution fusion | flops 550240256 | bytes 10776581 | tf_op jit(solution)/shard_map/while/body/eval_jaxpr/dot_general | solution.py:45
  59.9 0.1 convert_reduce_fusion.3
  59.9 0.1 broadcast_in_dim.81
  60.0 0.1 eq.93
  60.1 1.3 %fusion.31 = (f32[2048]{0:T(1024)S(1)}, f32[1024,2048]{1,0:T(8,128)S(1)}) fusion(s32[2048]{0:T(1024)S(1)} %eq.93, s32[1024]{0:T(1024)S(1)} %convert_reduce_fusion.3, bf16[2048,128]{1,0:T(8,128)(2,1)S(1)} %get-tuple-element.375, bf16[2048,128]{1,0:T(8,128)(2,1)S(1)} %get-tuple-element.374, s32[]{:T(128)S(6)} %select_n.63), kind=kOutput, calls=%fused_computation.3.clone.1 | convolution fusion | flops 545257472 | bytes 9195524 | tf_op jit(solution)/shard_map/while/body/eval_jaxpr/dot_general | solution.py:38
  61.4 2.7 %fusion.32 = f32[2048]{0:T(1024)S(1)} fusion(f32[1024,2048]{1,0:T(8,128)S(1)} %get-tuple-element.340, f32[2048]{0:T(1024)S(1)} %select_maximum_fusion.2, s32[2048]{0:T(1024)S(1)} %eq.93, s32[1024]{0:T(1024)S(1)} %convert_reduce_fusion.3), kind=kLoop, calls=%fused_computation.5.clone.1 | loop fusion | flops 12580864 | bytes 8417280 | tf_op jit(solution)/shard_map/while/body/eval_jaxpr/reduce_sum | solution.py:44
  64.1 2.8 %fusion.34 = f32[2048,128]{1,0:T(8,128)S(1)} fusion(f32[1024,2048]{1,0:T(8,128)S(1)} %get-tuple-element.340, f32[2048]{0:T(1024)S(1)} %select_maximum_fusion.2, s32[2048]{0:T(1024)S(1)} %eq.93, s32[1024]{0:T(1024)S(1)} %convert_reduce_fusion.3, f32[2048,128]{1,0:T(8,128)S(1)} %get-tuple-element.359, f32[2048]{0:T(1024)S(1)} %get-tuple-element.342, ...), kind=kOutput, calls=%fused_computation.7.clone.1 | convolution fusion | flops 550240256 | bytes 10776581 | tf_op jit(solution)/shard_map/while/body/eval_jaxpr/dot_general | solution.py:45
  67.0 0.3 divide_convert_fusion
  67.3 1.0 %reshape.47 = bf16[128,2048]{1,0:T(8,128)(2,1)} reshape(bf16[2048,128]{1,0:T(8,128)(2,1)S(1)} %divide_convert_fusion) | data formatting | bytes 1048576 | tf_op jit(solution)/shard_map/reshape | solution.py:66
  68.3 0.1 reshape.48
  68.4 0.7 copy.8
  (18 shorter events, 0.1 us)
Async XLA Ops:
  7.2 44.2 %all-gather.2.cloned.1.call-start = ((), (), s32[]{:S(2)}) async-start(), calls=%async_computation | async-start | bytes 1114112 | tf_op jit(solution)/shard_map/all_gather | solution.py:13
Sparse Core Ops, SparseCore 0:
  10.7 40.6 all-gather.1
